TPU v7x, 32 devices: a whole 2x2x4 slice. The times are simulated.
32 devices in a mesh: rows: 4 (over y, x), cand: 8 (over z, core).
Axes of the slice: x: 2, y: 2, z: 4, core: 2. Of those that a mesh axis runs over, the one named last changes fastest.
Arguments:
- whitened: float32 [256, 2048], P('cand', 'rows'), may hold values from -6 to 6
- factor_rows: float32 [2048, 2048], P('rows'), as said below
- diag_inv: float32 [2048, 512], P('rows'), as said below
- observed: float32 [22, 2048], P(None, 'rows'), may hold values from 0 to 1
- inv_length: float32 [22], replicated, may hold values from 0.4 to 2
- grid_coords: int32 [22, 32768], P(None, 'cand'), may hold values from 0 to 20
- frequencies: float32 [22, 8192], P(None, 'rows'), may hold values from -8 to 8
- phases: float32 [8192], P('rows'), may hold values from -3.140625 to 3.140625
- prior_coef: bfloat16 [256, 8192], P('cand', 'rows'), may hold values from -6 to 6
Outputs:
- samples_at: float32 [32768, 256], P('cand', 'rows')
Inputs may be any that keep to these rules, and one draw needn't show every extreme that they name: `factor_rows`: entries in and above the diagonal blocks of 512 x 512 are zero. `diag_inv`: each block of 512 rows is lower triangular with a positive diagonal.
All inputs are finite; a program needn't handle non-finite values.
Results may differ from a plain program's by a relative error of at most 0.004.
Values may be sent and summed in bfloat16 or wider, within the bound.
A program may use at most 320 MiB of HBM per device.

v0:
```python
import jax
import jax.numpy as jnp
from jax import lax
from jax.sharding import PartitionSpec as P

FEAT = 8192
GRID = 21


def from_behind(shard, axis, by):
    peers = lax.axis_size(axis)
    pairs = [(i, i + by) for i in range(peers) if 0 <= i + by < peers]
    return lax.ppermute(shard, axis, pairs)


def solve_chain(whitened, factor_rows, diag_inv):
    sections = lax.axis_size("rows")
    position = lax.axis_index("rows")
    rows_dev = factor_rows.shape[0]
    block_width = diag_inv.shape[1]
    offset = position * rows_dev
    carried = jnp.zeros((whitened.shape[0], factor_rows.shape[1]), jnp.float32)
    weights = jnp.zeros_like(whitened)

    def solve_own(state):
        incoming, earlier = state
        remaining = whitened - lax.dynamic_slice_in_dim(incoming, offset, rows_dev, 1)
        pieces = []
        for block_id in reversed(range(rows_dev // block_width)):
            first_col = block_id * block_width
            solved = jnp.dot(
                remaining[:, first_col : first_col + block_width],
                diag_inv,
                precision=lax.Precision.HIGHEST,
                preferred_element_type=jnp.float32,
            )
            own_columns = lax.dynamic_slice_in_dim(factor_rows, offset, rows_dev, 1)
            remaining = remaining - jnp.dot(
                solved,
                own_columns,
                precision=lax.Precision.HIGHEST,
                preferred_element_type=jnp.float32,
            )
            pieces.append(solved)
        solved_all = jnp.concatenate(pieces[::-1], axis=1)
        updated = incoming + jnp.dot(
            solved_all,
            factor_rows,
            precision=lax.Precision.HIGHEST,
            preferred_element_type=jnp.float32,
        )
        return (updated, solved_all)

    def pass_on(state):
        return state

    for section_id in range(sections):
        carried, weights = lax.cond(
            position == sections - 1 - section_id, solve_own, pass_on, (carried, weights)
        )
        if section_id + 1 < sections:
            carried = from_behind(carried, "rows", -1)
    return weights


def prior_slab(mixture, frequencies, phases, coef_slab):
    angles = (
        lax.dot_general(
            mixture,
            frequencies,
            (((0,), (0,)), ((), ())),
            precision=lax.Precision.HIGHEST,
            preferred_element_type=jnp.float32,
        )
        + phases[None, :]
    )
    features_map = (jnp.sqrt(2.0 / FEAT) * jnp.cos(angles)).astype(jnp.bfloat16)
    return lax.dot_general(
        features_map, coef_slab, (((1,), (1,)), ((), ())), preferred_element_type=jnp.float32
    )


def cross_part(mixture, observed, inv_length, weights_wire):
    squared = jnp.zeros((mixture.shape[1], observed.shape[1]), jnp.float32)
    for column in range(mixture.shape[0]):
        gap = (mixture[column][:, None] - observed[column][None, :]) * inv_length[column]
        squared = squared + gap * gap
    kernel_tile = jnp.exp(-0.5 * squared).astype(jnp.bfloat16)
    return lax.dot_general(
        kernel_tile, weights_wire, (((1,), (1,)), ((), ())), preferred_element_type=jnp.float32
    )


def body(
    whitened,
    factor_rows,
    diag_inv,
    observed,
    inv_length,
    grid_coords,
    frequencies,
    phases,
    prior_coef,
):
    coef_all = lax.all_gather(prior_coef, "cand", axis=0, tiled=True)
    weights = lax.all_gather(
        solve_chain(whitened, factor_rows, diag_inv).astype(jnp.bfloat16),
        "cand",
        axis=0,
        tiled=True,
    )
    mixture = grid_coords.astype(jnp.float32) / (GRID - 1)
    summed = prior_slab(mixture, frequencies, phases, coef_all) + cross_part(
        mixture, observed, inv_length, weights
    )
    return lax.psum_scatter(summed, "rows", scatter_dimension=1, tiled=True)


def solution(mesh):
    in_specs = (
        P("cand", "rows"),
        P("rows", None),
        P("rows", None),
        P(None, "rows"),
        P(),
        P(None, "cand"),
        P(None, "rows"),
        P("rows"),
        P("cand", "rows"),
    )
    out_specs = P("cand", "rows")
    return jax.shard_map(body, mesh=mesh, in_specs=in_specs, out_specs=out_specs, check_vma=False)
```

profile of v0, /device:TPU:0, one launch (start us, length us, event | category | flops | bytes accessed | tf_op | source)
XLA Modules:
  0.0 305.1 jit_solution(8331798818276321714)
XLA Ops:
  6.5 0.0 copy-start
  6.5 0.0 all-gather.2.cloned.1.call-start
  6.5 0.7 all-gather.2.cloned.1.call-update
  7.3 0.0 reduce-scatter.2.cloned.1.call-start
  7.3 0.7 conditional.4
  7.3 0.6 broadcast_in_dim.6
  8.0 1.3 collective-permute-start
  9.3 1.0 convert_multiply_fusion
  10.4 0.3 fusion.85
  10.6 0.8 fusion.88
  11.4 2.1 fusion.89
  13.5 1.4 fusion.90
  14.9 1.1 fusion.87
  16.1 3.0 collective-permute-done
  19.1 0.0 copy-start.3
  19.1 1.4 collective-permute-start.1
  20.5 44.7 %exponential_convert_fusion.4 = bf16[4096,512]{1,0:T(8,128)(2,1)} fusion(f32[]{:T(128)} %bitcast.65, f32[512]{0:T(512)S(1)} %bitcast.125, f32[4096]{0:T(1024)S(1)} %bitcast.104, f32[]{:T(128)} %bitcast.62, f32[512]{0:T(512)S(1)} %bitcast.126, f32[4096]{0:T(1024)S(1)} %bitcast.84, f32[]{:T(128)} %bitcast.59, f32[512]{0:T(512)S(1)} %bitcast.106, ...), kind=kLoop, calls=%fused_computation.18.clone.clone.1 | loop fusion | flops 186646528 | bytes 4599896 | tf_op jit(solution)/shard_map/dot_general | solution.py:89
  65.2 0.0 collective-permute-done.1
  65.2 0.0 copy-start.2
  65.2 0.0 copy-start.4
  65.2 0.0 copy-start.5
  65.2 1.6 collective-permute-start.2
  66.8 0.0 copy-done
  66.9 0.0 copy-done.3
  66.9 30.3 %fusion.84 = f32[4096,2048]{1,0:T(8,128)} fusion(f32[22,2048]{1,0:T(8,128)S(1)} %copy-done, s32[22,4096]{1,0:T(8,128)S(1)} %copy-done.3), kind=kOutput, calls=%fused_computation.90 | convolution fusion | flops 2214772736 | bytes 34095104 | tf_op jit(solution)/shard_map/dot_general | solution.py:68
  97.2 0.0 collective-permute-done.2
  97.2 0.0 copy-done.2
  97.2 0.0 copy-done.4
  97.2 1.4 conditional.7
  97.2 1.4 fusion.8
  98.6 0.8 convert_element_type.31
  99.4 14.7 %all_gather.7 = bf16[256,512]{1,0:T(8,128)(2,1)S(1)} all-gather(bf16[32,512]{1,0:T(8,128)(2,1)S(1)} %convert_element_type.31), channel_id=1, replica_groups=mesh['rows'=4,'cand'=8] {'cand'}, dimensions={0}, use_global_device_ids=true | all-gather | bytes 294912 | tf_op jit(solution)/shard_map/all_gather | solution.py:106
  114.1 0.0 all-gather.2.cloned.1.call-done
  114.1 0.0 copy-done.5
  114.1 0.0 copy-start.1
  114.1 113.2 %fusion.12 = f32[4096,256]{0,1:T(8,128)S(1)} fusion(bf16[256,2048]{1,0:T(8,128)(2,1)} %all-gather.2.cloned.1.call-done, f32[4096,2048]{1,0:T(8,128)} %fusion.84, f32[2048]{0:T(1024)S(1)} %copy-done.5), kind=kOutput, calls=%fused_computation.15 | convolution fusion | flops 4320133120 | bytes 38805504 | tf_op jit(solution)/shard_map/dot_general | solution.py:78
  227.3 0.0 copy-done.1
  227.3 3.4 %convolution_add_fusion.2 = f32[4096,256]{0,1:T(8,128)} fusion(f32[4096,256]{0,1:T(8,128)S(1)} %fusion.12, bf16[256,512]{1,0:T(8,128)(2,1)S(1)} %all_gather.7, bf16[4096,512]{1,0:T(8,128)(2,1)S(1)} %copy-done.1), kind=kOutput, calls=%fused_computation.19 | convolution fusion | flops 1074790400 | bytes 12845056 | tf_op jit(solution)/shard_map/dot_general | solution.py:89
  230.7 0.0 reduce-scatter.2.cloned.1.call-update
  230.7 67.5 %reduce-scatter.2.cloned.1.call-done = f32[4096,64]{0,1:T(8,128)} async-done(((f32[4096,256]{0,1:T(8,128)}), f32[4096,64]{0,1:T(8,128)}) %reduce-scatter.2.cloned.1.call-update) | async-done | bytes 1048592 | tf_op jit(solution)/shard_map/reduce_scatter | solution.py:116
  (4 shorter events, 0.1 us)
Async XLA Ops:
  6.5 60.3 %copy-start = (f32[22,2048]{1,0:T(8,128)S(1)}, f32[22,2048]{1,0:T(8,128)}, u32[]{:S(2)}) copy-start(f32[22,2048]{1,0:T(8,128)} %param.23) | copy-start | bytes 540676
  6.5 107.6 %all-gather.2.cloned.1.call-start = ((), (), s32[]{:S(2)}) async-start(), calls=%async_computation.1 | async-start | bytes 1179648 | tf_op jit(solution)/shard_map/all_gather | solution.py:105
  7.3 291.0 %reduce-scatter.2.cloned.1.call-start = ((), (), s32[]{:S(2)}) async-start(), calls=%async_computation.2 | async-start | bytes 5242880 | tf_op jit(solution)/shard_map/reduce_scatter | solution.py:116
  8.0 11.1 %collective-permute-start = (f32[32,2048]{1,0:T(8,128)S(1)}, f32[32,2048]{1,0:T(8,128)S(1)}, u32[]{:S(2)}, u32[]{:S(2)}) collective-permute-start(f32[32,2048]{1,0:T(8,128)S(1)} %get-tuple-element.77), channel_id=1, source_target_pairs={{8,0},{16,8},{24,16},{9,1},{17,9},{25,17},{10,2},{18,10},{26,18},{... | collective-permute-start | bytes 786440 | tf_op jit(solution)/shard_map/ppermute | solution.py:13
  19.1 47.7 %copy-start.3 = (s32[22,4096]{1,0:T(8,128)S(1)}, s32[22,4096]{1,0:T(8,128)}, u32[]{:S(2)}) copy-start(s32[22,4096]{1,0:T(8,128)} %param.22) | copy-start | bytes 1081348
  19.1 46.1 %collective-permute-start.1 = (f32[32,2048]{1,0:T(8,128)S(1)}, f32[32,2048]{1,0:T(8,128)S(1)}, u32[]{:S(2)}, u32[]{:S(2)}) collective-permute-start(f32[32,2048]{1,0:T(8,128)S(1)} %get-tuple-element.79), channel_id=1, source_target_pairs={{8,0},{16,8},{24,16},{9,1},{17,9},{25,17},{10,2},{18,10},{26,18},{... | collective-permute-start | bytes 786440 | tf_op jit(solution)/shard_map/ppermute | solution.py:13
  65.2 32.0 %copy-start.2 = (f32[512,512]{1,0:T(8,128)S(1)}, f32[512,512]{1,0:T(8,128)}, u32[]{:S(2)}) copy-start(f32[512,512]{1,0:T(8,128)} %param.19) | copy-start | bytes 3145732
  65.2 32.0 %copy-start.4 = (f32[32,512]{1,0:T(8,128)S(1)}, f32[32,512]{1,0:T(8,128)}, u32[]{:S(2)}) copy-start(f32[32,512]{1,0:T(8,128)} %param.17) | copy-start | bytes 196612
  65.2 48.9 %copy-start.5 = (f32[2048]{0:T(1024)S(1)}, f32[2048]{0:T(1024)}, u32[]{:S(2)}) copy-start(f32[2048]{0:T(1024)} %param.24) | copy-start | bytes 24580
  65.2 32.0 %collective-permute-start.2 = (f32[32,2048]{1,0:T(8,128)S(1)}, f32[32,2048]{1,0:T(8,128)S(1)}, u32[]{:S(2)}, u32[]{:S(2)}) collective-permute-start(f32[32,2048]{1,0:T(8,128)S(1)} %get-tuple-element.82), channel_id=1, source_target_pairs={{8,0},{16,8},{24,16},{9,1},{17,9},{25,17},{10,2},{18,10},{26,18},{... | collective-permute-start | bytes 786440 | tf_op jit(solution)/shard_map/ppermute | solution.py:13
  114.1 113.2 %copy-start.1 = (bf16[4096,512]{1,0:T(8,128)(2,1)S(1)}, bf16[4096,512]{1,0:T(8,128)(2,1)}, u32[]{:S(2)}) copy-start(bf16[4096,512]{1,0:T(8,128)(2,1)} %exponential_convert_fusion.4) | copy-start | bytes 12582916
Sparse Core Ops, SparseCore 0:
  9.0 24.7 all-gather.1
  230.9 67.3 reduce-scatter.1
where the time goes:
time: 306 us; the launch traced here: 305 us
  matrix products  148 us (48%)
  waiting for transfers between devices  71.2 us (23%)
  other arithmetic  46.5 us (15%)
  blocking collectives  14.7 us (5%)
  between operations  13.5 us (4%)
  local copies, waits for them, and re-layouts  6.44 us (2%)
  starting transfers between devices  4.34 us (1%)
    dot_general x1, matrix products, prior_slab(): lax.dot_general(features_map, coef_slab, (((1,), (1,)), ((), ())), prefer...  113 us
    reduce_scatter x1, waiting for transfers between devices, body(): return lax.psum_scatter(summed, 'rows', scatter_dimension=1, tiled=True)  67.5 us
    dot_general x1, other arithmetic, cross_part(): lax.dot_general(kernel_tile, weights_wire, (((1,), (1,)), ((), ())), pref...  44.7 us
    dot_general x1, matrix products, prior_slab(): lax.dot_general(mixture, frequencies, (((0,), (0,)), ((), ())), precision...  30.3 us
    all_gather x1, blocking collectives, body(): lax.all_gather(solve_chain(whitened, factor_rows, diag_inv).astype(jnp.bf...  14.7 us
  transfers between devices with their start and end apart: 5, of which 2 were waited for; matrix products, arithmetic and copies ran while one was open for 28% of the time, Pallas kernels for 0%

commit v1 on v0

v1 whole, which is shorter than its diff:
```python
import functools

import jax
import jax.numpy as jnp
import numpy as np
from jax import lax
from jax.experimental import pallas as pl
from jax.experimental.pallas import tpu as pltpu
from jax.sharding import PartitionSpec as P

GRID = 21
CHUNK = 512
FB = 256
DEPTH = 128
HIGH = lax.Precision.HIGHEST
F32 = jnp.float32
BF16 = jnp.bfloat16


def sine_coefficients(terms):
    v = 0.125 * (1 - np.cos(np.pi * (np.arange(400) + 0.5) / 400)) + 1e-9
    rows = np.stack([v ** (2 * i + 1) for i in range(terms)], 1)
    goal = np.sin(2 * np.pi * v)
    return np.linalg.lstsq(rows / goal[:, None], np.ones_like(goal), rcond=None)[0]


def kernel(
    peers_r,
    peers_c,
    scale,
    g_ref,
    ft_ref,
    ot_ref,
    coef_ref,
    x_ref,
    fac_ref,
    dinv_ref,
    out_ref,
    feat,
    coefw,
    cbuf,
    wown,
    wbuf,
    wide,
    csend,
    crecv,
    acc,
    own,
    sbuf,
    rbuf,
    gs,
    gr,
    ws,
    wr,
    cs,
    cr,
    ss,
    sr,
):
    me = lax.axis_index("rows")
    c = lax.axis_index("cand")
    groups = peers_c // 2
    q = c // 2
    core = c % 2
    sibling = q * 2 + (1 - core)
    samples = coef_ref.shape[0]
    nf = ft_ref.shape[0] // FB
    no = ot_ref.shape[0] // FB
    slots = feat.shape[0]
    chunks = out_ref.shape[1] // CHUNK
    part = out_ref.shape[0]
    width = x_ref.shape[1]
    poly = [float(a) * scale for a in sine_coefficients(4)]

    barrier = pltpu.get_barrier_semaphore()
    for d in range(1, peers_r):
        pl.semaphore_signal(
            barrier, inc=1, device_id={"rows": (me + d) % peers_r}, device_id_type=pl.DeviceIdType.MESH
        )
    for d in range(1, groups):
        pl.semaphore_signal(
            barrier,
            inc=1,
            device_id={"cand": ((q + d) % groups) * 2 + core},
            device_id_type=pl.DeviceIdType.MESH,
        )
    pl.semaphore_signal(barrier, inc=1, device_id={"cand": sibling}, device_id_type=pl.DeviceIdType.MESH)
    pl.semaphore_wait(barrier, peers_r - 1 + groups)

    def hop(src, dst, send, recv, cand):
        return pltpu.make_async_remote_copy(
            src_ref=src,
            dst_ref=dst,
            send_sem=send,
            recv_sem=recv,
            device_id={"cand": cand},
            device_id_type=pl.DeviceIdType.MESH,
        )

    def gather_send(mine, buf, send, recv):
        for d in range(1, groups):
            hop(mine, buf.at[c], send.at[d], recv.at[c], ((q + d) % groups) * 2 + core).start()
        hop(mine, buf.at[c], send.at[groups], recv.at[c], sibling).start()
        buf[c] = mine[...]

    def gather_forward(mine, buf, send, recv):
        for d in range(1, groups):
            other = ((q + groups - d) % groups) * 2 + core
            hop(mine, buf.at[other], send.at[d], recv.at[other], sibling).wait_recv()
            hop(buf.at[other], buf.at[other], send.at[groups + d], recv.at[other], sibling).start()

    def gather_finish(mine, buf, send, recv):
        for d in range(groups):
            other = ((q + groups - d) % groups) * 2 + (1 - core)
            hop(mine, buf.at[other], send.at[d], recv.at[other], sibling).wait_recv()
        for d in range(1, 2 * groups):
            hop(mine, buf.at[c], send.at[d], recv.at[c], sibling).wait_send()

    def chain(i, source):
        return pltpu.make_async_remote_copy(
            src_ref=csend.at[i],
            dst_ref=crecv.at[source],
            send_sem=cs.at[i],
            recv_sem=cr.at[source],
            device_id={"rows": i},
            device_id_type=pl.DeviceIdType.MESH,
        )

    def stage(s):
        @pl.when(me == s)
        def _():
            x = x_ref[...]
            for j in range(peers_r - 1, s, -1):
                chain(s, j).wait_recv()
                x = x - crecv[j]
            w = jnp.dot(x, dinv_ref[...], precision=HIGH, preferred_element_type=F32)
            wown[...] = w.astype(BF16)
            for i in range(s - 1, -1, -1):
                csend[i] = jnp.dot(
                    w, fac_ref[:, i * width : (i + 1) * width], precision=HIGH, preferred_element_type=F32
                )
                chain(i, s).start()

    def cos_block(k, j, slot):
        rows = pl.ds(pl.multiple_of(j * FB, FB), FB)
        turns = jnp.dot(
            ft_ref[rows, :],
            g_ref[:, pl.ds(pl.multiple_of(k * CHUNK, CHUNK), CHUNK)],
            preferred_element_type=F32,
        )
        v = 0.25 - jnp.abs(turns - jnp.round(turns))
        u = v * v
        p = poly[3]
        for a in (poly[2], poly[1], poly[0]):
            p = p * u + a
        feat[slot, rows, :] = (p * v).astype(BF16)

    def exp_block(k, j, slot):
        turns = jnp.dot(
            ot_ref[pl.ds(pl.multiple_of(j * FB, FB), FB), :],
            g_ref[:, pl.ds(pl.multiple_of(k * CHUNK, CHUNK), CHUNK)],
            preferred_element_type=F32,
        )
        feat[slot, pl.ds(pl.multiple_of((j + nf) * FB, FB), FB), :] = jnp.exp2(turns).astype(BF16)

    def product(j, slot):
        cols = pl.ds(pl.multiple_of(j * FB, FB), FB)
        acc[...] += jnp.dot(coefw[:, cols], feat[slot, cols, :], preferred_element_type=F32)

    def features(k):
        pl.loop(0, nf)(lambda j: cos_block(k, j, k % slots))
        pl.loop(0, no)(lambda j: exp_block(k, j, k % slots))

    def share(k, to, source):
        return pltpu.make_async_remote_copy(
            src_ref=sbuf.at[k, to],
            dst_ref=rbuf.at[k, source],
            send_sem=ss.at[k, to],
            recv_sem=sr.at[k, source],
            device_id={"rows": to},
            device_id_type=pl.DeviceIdType.MESH,
        )

    def deliver(k):
        own[k] = acc[pl.ds(pl.multiple_of(me * part, part), part), :]
        for d in range(1, peers_r):
            to = (me + d) % peers_r
            sbuf[k, to] = acc[pl.ds(pl.multiple_of(to * part, part), part), :].astype(BF16)
            share(k, to, me).start()

    gather_send(coef_ref, cbuf, gs, gr)
    for s in range(peers_r - 1, -1, -1):
        stage(s)
        if s == 0:
            gather_send(wown, wbuf, ws, wr)
            gather_forward(coef_ref, cbuf, gs, gr)
        if peers_r - 1 - s < slots:
            features(peers_r - 1 - s)
    gather_forward(wown, wbuf, ws, wr)
    gather_finish(coef_ref, cbuf, gs, gr)
    for b in range(peers_c):
        wide[b * samples : (b + 1) * samples, : nf * FB] = cbuf[b].astype(F32)
    gather_finish(wown, wbuf, ws, wr)
    for b in range(peers_c):
        wide[b * samples : (b + 1) * samples, nf * FB :] = wbuf[b].astype(F32)
    coefw[...] = wide[...].astype(BF16)

    @pl.loop(0, chunks - slots)
    def _(k):
        slot = k % slots
        acc[...] = jnp.zeros_like(acc)

        @pl.loop(0, nf)
        def _(j):
            product(j, slot)
            cos_block(k + slots, j, slot)

        @pl.loop(0, no)
        def _(j):
            product(j + nf, slot)
            exp_block(k + slots, j, slot)

        deliver(k)

    @pl.loop(chunks - slots, chunks)
    def _(k):
        acc[...] = jnp.dot(coefw[...], feat[k % slots], preferred_element_type=F32)
        deliver(k)

    @pl.loop(0, chunks)
    def _(k):
        total = own[k]
        for d in range(1, peers_r):
            source = (me + d) % peers_r
            share(k, source, source).wait_recv()
            total = total + rbuf[k, source].astype(F32)
        out_ref[:, pl.ds(pl.multiple_of(k * CHUNK, CHUNK), CHUNK)] = total
        for d in range(1, peers_r):
            to = (me + d) % peers_r
            share(k, to, me).wait_send()

    for i in range(peers_r - 1):

        @pl.when(me > i)
        def _():
            chain(i, me).wait_send()


def rounded(a):
    return lax.reduce_precision(a, exponent_bits=8, mantissa_bits=7)


def pieces(a):
    first = rounded(a)
    second = rounded(a - first)
    return [first, second, rounded(a - first - second)]


def padded(rows):
    stacked = jnp.concatenate(rows, axis=0)
    return jnp.pad(stacked, ((0, DEPTH - stacked.shape[0]), (0, 0))).astype(BF16)


def body(whitened, factor_rows, diag_inv, observed, inv_length, grid_coords, frequencies, phases, prior_coef):
    peers_r = lax.axis_size("rows")
    peers_c = lax.axis_size("cand")
    feats = frequencies.shape[1]
    obs = observed.shape[1]
    cands = grid_coords.shape[1]
    samples, width = whitened.shape
    all_samples = samples * peers_c
    part = all_samples // peers_r
    chunks = cands // CHUNK
    slots = 4
    top = GRID - 1
    turn = 1.0 / (2 * np.pi)
    log2e = 1.0 / np.log(2.0)

    levels = grid_coords.astype(F32)
    l2 = (inv_length * inv_length)[:, None]
    per_cand = jnp.sum(levels * levels * l2, axis=0, keepdims=True) * (-0.5 * log2e / (top * top))
    per_obs = jnp.sum(observed * observed * l2, axis=0, keepdims=True) * (-0.5 * log2e)
    ones = jnp.ones((3, cands), F32)
    g = padded([levels, levels, levels, ones] + pieces(per_cand))
    ft = padded(pieces(frequencies * (turn / top)) + pieces(phases[None, :] * turn)).T
    ot = padded(
        pieces(observed * l2 * (log2e / top)) + pieces(per_obs) + [jnp.ones((3, obs), F32)]
    ).T
    scale = float(np.sqrt(2.0 / (feats * peers_r)))

    vmem = pl.BlockSpec(memory_space=pltpu.VMEM)
    dma = pltpu.SemaphoreType.DMA
    out = pl.pallas_call(
        functools.partial(kernel, peers_r, peers_c, scale),
        out_shape=jax.ShapeDtypeStruct((part, cands), F32),
        in_specs=[vmem] * 7,
        out_specs=vmem,
        scratch_shapes=[
            pltpu.VMEM((slots, feats + obs, CHUNK), BF16),
            pltpu.VMEM((all_samples, feats + obs), BF16),
            pltpu.VMEM((peers_c, samples, feats), BF16),
            pltpu.VMEM((samples, width), BF16),
            pltpu.VMEM((peers_c, samples, width), BF16),
            pltpu.VMEM((all_samples, feats + obs), F32),
            pltpu.VMEM((peers_r, samples, width), F32),
            pltpu.VMEM((peers_r, samples, width), F32),
            pltpu.VMEM((all_samples, CHUNK), F32),
            pltpu.VMEM((chunks, part, CHUNK), F32),
            pltpu.VMEM((chunks, peers_r, part, CHUNK), BF16),
            pltpu.VMEM((chunks, peers_r, part, CHUNK), BF16),
            dma((peers_c,)),
            dma((peers_c,)),
            dma((peers_c,)),
            dma((peers_c,)),
            dma((peers_r,)),
            dma((peers_r,)),
            dma((chunks, peers_r)),
            dma((chunks, peers_r)),
        ],
        compiler_params=pltpu.CompilerParams(
            collective_id=0, has_side_effects=True, vmem_limit_bytes=56 * 1024 * 1024
        ),
    )(g, ft, ot, prior_coef, whitened, factor_rows, diag_inv)
    return out.T


def solution(mesh):
    in_specs = (
        P("cand", "rows"),
        P("rows", None),
        P("rows", None),
        P(None, "rows"),
        P(),
        P(None, "cand"),
        P(None, "rows"),
        P("rows"),
        P("cand", "rows"),
    )
    out_specs = P("cand", "rows")
    return jax.shard_map(body, mesh=mesh, in_specs=in_specs, out_specs=out_specs, check_vma=False)
```

time: 306 us -> 79.8 us (0.26)
  matrix products: 148 us -> 0 us
  waiting for transfers between devices: 71.2 us -> 0 us
  Pallas kernels: 0 us -> 63.7 us
  other arithmetic: 46.5 us -> 2.25 us
  blocking collectives: 14.7 us -> 0 us
  between operations: 13.5 us -> 0.17 us
  local copies, waits for them, and re-layouts: 6.44 us -> 13.3 us
  starting transfers between devices: 4.34 us -> 0 us
    dot_general x4 -> x0, matrix products: 148 us -> none  [the longest x1 113 us: prior_slab(): lax.dot_general(features_map, coef_slab, (((1,), (1,)), ((), ())), prefer...]
    reduce_scatter x1 -> x0, waiting for transfers between devices: 67.5 us -> none  [body(): return lax.psum_scatter(summed, 'rows', scatter_dimension=1, tiled=True)]
    pallas_call x0 -> x1, Pallas kernels: none -> 63.7 us  [body(): pl.pallas_call(functools.partial(kernel, peers_r, peers_c, scale), out_sh...]
    dot_general x1 -> x0, other arithmetic: 44.7 us -> none  [cross_part(): lax.dot_general(kernel_tile, weights_wire, (((1,), (1,)), ((), ())), pref...]
    all_gather x1 -> x0, blocking collectives: 14.7 us -> none  [body(): lax.all_gather(solve_chain(whitened, factor_rows, diag_inv).astype(jnp.bf...]
    slice x6 -> x0, local copies, waits for them, and re-layouts: 5.75 us -> none  [the longest x2 3.49 us: cross_part(): inv_length[column]]
    unnamed x12 -> x7, local copies, waits for them, and re-layouts: 0.03 us -> 4.48 us
    ppermute x3 -> x0, starting transfers between devices: 4.3 us -> none  [from_behind(): return lax.ppermute(shard, axis, pairs)]
  transfers between devices with their start and end apart: 5 -> 0, of which waited for: 2 -> 0; matrix products, arithmetic and copies ran while one was open for 28% -> 0% of each run, Pallas kernels for 0% -> 0%
where the time goes in v1:
time: 79.8 us; the launch traced here: 79.4 us
  Pallas kernels  63.7 us (80%)
  local copies, waits for them, and re-layouts  13.3 us (17%)
  other arithmetic  2.25 us (3%)
    pallas_call x1, Pallas kernels, body(): pl.pallas_call(functools.partial(kernel, peers_r, peers_c, scale), out_sh...  63.7 us
    unnamed x7, local copies, waits for them, and re-layouts  4.48 us
    concatenate x3, local copies, waits for them, and re-layouts, padded(): stacked = jnp.concatenate(rows, axis=0)  3.64 us
    transpose x1, local copies, waits for them, and re-layouts, body(): padded(pieces(frequencies * (turn / top)) + pieces(phases[None, :] * turn))  1.94 us

profile of v1, /device:TPU:0, one launch (start us, length us, event | category | flops | bytes accessed | tf_op | source)
XLA Modules:
  0.0 79.4 jit_solution(13452939127345383608)
XLA Ops:
  0.0 0.0 copy-start.1
  0.0 0.7 mul.101
  0.7 0.9 %multiply_reduce_fusion.1 = f32[512]{0:T(512)S(1)} fusion(f32[22,512]{1,0:T(8,128)} %param.12, f32[22]{0:T(128)S(1)} %mul.101), kind=kLoop, calls=%fused_computation.21 | loop fusion | flops 33280 | bytes 47192 | tf_op jit(solution)/shard_map/reduce_sum | solution.py:282
  1.6 0.1 copy.31
  1.8 0.1 copy.30
  1.9 0.1 fusion.5
  2.0 0.9 %copy.28 = f32[22,512]{0,1:T(8,128)S(1)} copy(f32[22,512]{1,0:T(8,128)} %param.12) | data formatting | bytes 90112 | tf_op args[3]
  3.0 0.1 fusion.3
  3.0 0.2 copy.32
  3.3 0.3 concatenate.14
  3.6 0.7 pad_bitcast_fusion.1.ot_ref
  4.3 1.3 %copy.23 = f32[22,2048]{0,1:T(8,128)S(1)} copy(f32[22,2048]{1,0:T(8,128)} %param.15) | data formatting | bytes 360448 | tf_op args[6]
  5.6 0.0 copy-start
  5.6 0.3 fusion.1
  5.9 0.0 copy-done.1
  5.9 0.3 reduce_precision.144
  6.2 0.3 reduce_precision.145
  6.6 0.3 reduce_precision.146
  6.9 2.3 %concatenate.13 = bf16[69,2048]{0,1:T(8,128)(2,1)} concatenate(bf16[22,2048]{0,1:T(8,128)(2,1)S(1)} %get-tuple-element.7, bf16[22,2048]{0,1:T(8,128)(2,1)S(1)} %get-tuple-element.6, bf16[22,2048]{0,1:T(8,128)(2,1)S(1)} %get-tuple-element.5, bf16[1,2048]{0,1:T(8,128)(2,1)S(1)} %reduce_precision.144, bf16[1,2048]{0,1:T(8,128)(2,1)S(1)} %reduce_precision.145, ...), dimensions={0} | concatenate | bytes 565248 | tf_op jit(solution)/shard_map/concatenate | solution.py:260
  9.3 1.9 %pad_bitcast_fusion.ft_ref = bf16[2048,128]{1,0:T(8,128)(2,1)} fusion(bf16[69,2048]{0,1:T(8,128)(2,1)} %concatenate.13), kind=kLoop, calls=%fused_computation.6 | loop fusion | bytes 806912 | tf_op jit(solution)/shard_map/transpose | solution.py:285
  11.2 0.0 copy-done
  11.2 0.1 multiply_reduce_fusion
  11.4 0.9 %concatenate.12 = bf16[72,4096]{1,0:T(8,128)(2,1)S(1)} concatenate(bf16[22,4096]{1,0:T(8,128)(2,1)S(1)} %convert_convert_fusion, bf16[22,4096]{1,0:T(8,128)(2,1)S(1)} %convert_convert_fusion, bf16[22,4096]{1,0:T(8,128)(2,1)S(1)} %convert_convert_fusion, bf16[3,4096]{1,0:T(4,128)(2,1)S(1)} %broadcast_in_dim.4, bf16[1,4096]{1,0:T(2,128)(2,1)S(1)} %get-tuple-element.15, ...), dimensions={0} | concatenate | bytes 1179648 | tf_op jit(solution)/shard_map/concatenate | solution.py:260
  12.4 1.0 %pad.15.g_ref = bf16[128,4096]{1,0:T(8,128)(2,1)} pad(bf16[72,4096]{1,0:T(8,128)(2,1)S(1)} %concatenate.12, bf16[]{:T(256)} %constant.5.clone.1), padding=0_56x0_0 | pad | bytes 1638402 | tf_op jit(solution)/shard_map/jit(_pad)/pad | solution.py:261
  13.4 63.7 %shard_map.91 = f32[64,4096]{1,0:T(8,128)} custom-call(bf16[128,4096]{1,0:T(8,128)(2,1)} %pad.15.g_ref, bf16[2048,128]{1,0:T(8,128)(2,1)} %pad_bitcast_fusion.ft_ref, bf16[512,128]{1,0:T(8,128)(2,1)} %pad_bitcast_fusion.1.ot_ref, bf16[32,2048]{1,0:T(8,128)(2,1)} %coef_ref.1, f32[32,512]{1,0:T(8,128)} %x_ref.1, f32[512,2048]{1,0:T(8,128)} %fac_ref.1, ...), custom_call_target="tpu_custom_call" | custom-call | tf_op jit(solution)/shard_map/pallas_call | solution.py:293
  77.1 2.3 %copy.34 = f32[4096,64]{0,1:T(8,128)} copy(f32[4096,64]{0,1:T(8,128)} %bitcast.7) | data formatting | bytes 2097152
  (8 shorter events, 0.1 us)
Async XLA Ops:
  0.0 5.9 %copy-start.1 = (f32[2048]{0:T(1024)S(1)}, f32[2048]{0:T(1024)}, u32[]{:S(2)}) copy-start(f32[2048]{0:T(1024)} %param.16) | copy-start | bytes 24580
  5.6 5.6 %copy-start = (s32[22,4096]{1,0:T(8,128)S(1)}, s32[22,4096]{1,0:T(8,128)}, u32[]{:S(2)}) copy-start(s32[22,4096]{1,0:T(8,128)} %param.14) | copy-start | bytes 1081348

commit v2 on v1

--- a/solution.py
+++ b/solution.py
@@ -11,7 +11,10 @@
 GRID = 21
 CHUNK = 512
 FB = 256
+FW = 1024
+EW = 512
 DEPTH = 128
+SEG = 32
 HIGH = lax.Precision.HIGHEST
 F32 = jnp.float32
 BF16 = jnp.bfloat16
@@ -24,24 +27,36 @@
     return np.linalg.lstsq(rows / goal[:, None], np.ones_like(goal), rcond=None)[0]
 
 
+def pieces(a):
+    first = a.astype(BF16).astype(F32)
+    second = (a - first).astype(BF16).astype(F32)
+    return [first, second, (a - first - second).astype(BF16).astype(F32)]
+
+
 def kernel(
     peers_r,
     peers_c,
     scale,
-    g_ref,
-    ft_ref,
-    ot_ref,
+    levels_ref,
+    obs_ref,
+    scale_ref,
+    freq_ref,
+    phase_ref,
     coef_ref,
     x_ref,
     fac_ref,
     dinv_ref,
     out_ref,
+    g_ref,
+    ft_ref,
+    ot_ref,
+    ctmp,
+    ttmp,
     feat,
     coefw,
     cbuf,
     wown,
     wbuf,
-    wide,
     csend,
     crecv,
     acc,
@@ -64,8 +79,8 @@
     core = c % 2
     sibling = q * 2 + (1 - core)
     samples = coef_ref.shape[0]
-    nf = ft_ref.shape[0] // FB
-    no = ot_ref.shape[0] // FB
+    feats = ft_ref.shape[0]
+    obs = ot_ref.shape[0]
     slots = feat.shape[0]
     chunks = out_ref.shape[1] // CHUNK
     part = out_ref.shape[0]
@@ -141,35 +156,35 @@
                 )
                 chain(i, s).start()
 
-    def cos_block(k, j, slot):
-        rows = pl.ds(pl.multiple_of(j * FB, FB), FB)
-        turns = jnp.dot(
-            ft_ref[rows, :],
+    def angles(k, source, start, size):
+        return jnp.dot(
+            source[pl.ds(start, size), :],
             g_ref[:, pl.ds(pl.multiple_of(k * CHUNK, CHUNK), CHUNK)],
             preferred_element_type=F32,
         )
+
+    def cos_block(k, j, slot):
+        start = pl.multiple_of(j * FW, FW)
+        turns = angles(k, ft_ref, start, FW)
         v = 0.25 - jnp.abs(turns - jnp.round(turns))
         u = v * v
         p = poly[3]
         for a in (poly[2], poly[1], poly[0]):
             p = p * u + a
-        feat[slot, rows, :] = (p * v).astype(BF16)
+        feat[slot, pl.ds(start, FW), :] = (p * v).astype(BF16)
 
     def exp_block(k, j, slot):
-        turns = jnp.dot(
-            ot_ref[pl.ds(pl.multiple_of(j * FB, FB), FB), :],
-            g_ref[:, pl.ds(pl.multiple_of(k * CHUNK, CHUNK), CHUNK)],
-            preferred_element_type=F32,
-        )
-        feat[slot, pl.ds(pl.multiple_of((j + nf) * FB, FB), FB), :] = jnp.exp2(turns).astype(BF16)
-
-    def product(j, slot):
-        cols = pl.ds(pl.multiple_of(j * FB, FB), FB)
+        start = pl.multiple_of(j * EW, EW)
+        turns = angles(k, ot_ref, start, EW)
+        feat[slot, pl.ds(pl.multiple_of(feats + start, EW), EW), :] = jnp.exp2(turns).astype(BF16)
+
+    def product(start, size, slot):
+        cols = pl.ds(pl.multiple_of(start, size), size)
         acc[...] += jnp.dot(coefw[:, cols], feat[slot, cols, :], preferred_element_type=F32)
 
     def features(k):
-        pl.loop(0, nf)(lambda j: cos_block(k, j, k % slots))
-        pl.loop(0, no)(lambda j: exp_block(k, j, k % slots))
+        pl.loop(0, feats // FW)(lambda j: cos_block(k, j, k % slots))
+        pl.loop(0, obs // EW)(lambda j: exp_block(k, j, k % slots))
 
     def share(k, to, source):
         return pltpu.make_async_remote_copy(
@@ -189,6 +204,52 @@
             share(k, to, me).start()
 
     gather_send(coef_ref, cbuf, gs, gr)
+
+    dim = levels_ref.shape[0]
+    top = GRID - 1
+    turn = 1.0 / (2 * np.pi)
+    log2e = 1.0 / np.log(2.0)
+    l2 = scale_ref[...] * scale_ref[...]
+    ctmp[...] = jnp.zeros_like(ctmp)
+    ttmp[...] = jnp.zeros_like(ttmp)
+
+    @pl.loop(0, feats // FB)
+    def _(j):
+        cols = pl.ds(pl.multiple_of(j * FB, FB), FB)
+        for i, piece in enumerate(pieces(freq_ref[:, cols] * (turn / top))):
+            ttmp[SEG * i : SEG * i + dim, :] = piece
+        for i, piece in enumerate(pieces(phase_ref[:, cols] * turn)):
+            ttmp[3 * SEG + i : 3 * SEG + i + 1, :] = piece
+        ft_ref[cols, :] = jnp.transpose(ttmp[...]).astype(BF16)
+
+    ttmp[3 * SEG + 3 : 3 * SEG + 6, :] = jnp.ones((3, FB), F32)
+
+    @pl.loop(0, obs // FB)
+    def _(j):
+        cols = pl.ds(pl.multiple_of(j * FB, FB), FB)
+        seen = obs_ref[:, cols]
+        for i, piece in enumerate(pieces(seen * l2 * (log2e / top))):
+            ttmp[SEG * i : SEG * i + dim, :] = piece
+        norm = jnp.sum(seen * seen * l2, axis=0, keepdims=True) * (-0.5 * log2e)
+        for i, piece in enumerate(pieces(norm)):
+            ttmp[3 * SEG + i : 3 * SEG + i + 1, :] = piece
+        ot_ref[cols, :] = jnp.transpose(ttmp[...]).astype(BF16)
+
+    @pl.loop(0, chunks)
+    def _(k):
+        cols = pl.ds(pl.multiple_of(k * CHUNK, CHUNK), CHUNK)
+        levels = levels_ref[:, cols].astype(F32)
+        ctmp[0:dim, :] = levels
+        low = ctmp[...].astype(BF16)
+        norm = jnp.sum(levels * levels * l2, axis=0, keepdims=True) * (-0.5 * log2e / (top * top))
+        row = lax.broadcasted_iota(jnp.int32, (SEG, CHUNK), 0)
+        tail = jnp.where(row < 3, 1.0, 0.0)
+        for i, piece in enumerate(pieces(norm)):
+            tail = jnp.where(row == 3 + i, piece, tail)
+        for i in range(3):
+            g_ref[SEG * i : SEG * (i + 1), cols] = low
+        g_ref[3 * SEG :, cols] = tail.astype(BF16)
+
     for s in range(peers_r - 1, -1, -1):
         stage(s)
         if s == 0:
@@ -198,26 +259,28 @@
             features(peers_r - 1 - s)
     gather_forward(wown, wbuf, ws, wr)
     gather_finish(coef_ref, cbuf, gs, gr)
-    for b in range(peers_c):
-        wide[b * samples : (b + 1) * samples, : nf * FB] = cbuf[b].astype(F32)
     gather_finish(wown, wbuf, ws, wr)
-    for b in range(peers_c):
-        wide[b * samples : (b + 1) * samples, nf * FB :] = wbuf[b].astype(F32)
-    coefw[...] = wide[...].astype(BF16)
+    for buf, cols in ((cbuf, slice(0, feats)), (wbuf, slice(feats, feats + obs))):
+        for b in range(0, peers_c, max(1, 16 // samples)):
+            if samples % 16 == 0:
+                coefw[b * samples : (b + 1) * samples, cols] = buf[b]
+            else:
+                group = [buf[b + i].astype(F32) for i in range(16 // samples)]
+                coefw[b * samples : b * samples + 16, cols] = jnp.concatenate(group, axis=0).astype(BF16)
 
     @pl.loop(0, chunks - slots)
     def _(k):
         slot = k % slots
         acc[...] = jnp.zeros_like(acc)
 
-        @pl.loop(0, nf)
+        @pl.loop(0, feats // FW)
         def _(j):
-            product(j, slot)
+            product(j * FW, FW, slot)
             cos_block(k + slots, j, slot)
 
-        @pl.loop(0, no)
+        @pl.loop(0, obs // EW)
         def _(j):
-            product(j + nf, slot)
+            product(feats + j * EW, EW, slot)
             exp_block(k + slots, j, slot)
 
         deliver(k)
@@ -246,21 +309,6 @@
             chain(i, me).wait_send()
 
 
-def rounded(a):
-    return lax.reduce_precision(a, exponent_bits=8, mantissa_bits=7)
-
-
-def pieces(a):
-    first = rounded(a)
-    second = rounded(a - first)
-    return [first, second, rounded(a - first - second)]
-
-
-def padded(rows):
-    stacked = jnp.concatenate(rows, axis=0)
-    return jnp.pad(stacked, ((0, DEPTH - stacked.shape[0]), (0, 0))).astype(BF16)
-
-
 def body(whitened, factor_rows, diag_inv, observed, inv_length, grid_coords, frequencies, phases, prior_coef):
     peers_r = lax.axis_size("rows")
     peers_c = lax.axis_size("cand")
@@ -272,20 +320,6 @@
     part = all_samples // peers_r
     chunks = cands // CHUNK
     slots = 4
-    top = GRID - 1
-    turn = 1.0 / (2 * np.pi)
-    log2e = 1.0 / np.log(2.0)
-
-    levels = grid_coords.astype(F32)
-    l2 = (inv_length * inv_length)[:, None]
-    per_cand = jnp.sum(levels * levels * l2, axis=0, keepdims=True) * (-0.5 * log2e / (top * top))
-    per_obs = jnp.sum(observed * observed * l2, axis=0, keepdims=True) * (-0.5 * log2e)
-    ones = jnp.ones((3, cands), F32)
-    g = padded([levels, levels, levels, ones] + pieces(per_cand))
-    ft = padded(pieces(frequencies * (turn / top)) + pieces(phases[None, :] * turn)).T
-    ot = padded(
-        pieces(observed * l2 * (log2e / top)) + pieces(per_obs) + [jnp.ones((3, obs), F32)]
-    ).T
     scale = float(np.sqrt(2.0 / (feats * peers_r)))
 
     vmem = pl.BlockSpec(memory_space=pltpu.VMEM)
@@ -293,15 +327,19 @@
     out = pl.pallas_call(
         functools.partial(kernel, peers_r, peers_c, scale),
         out_shape=jax.ShapeDtypeStruct((part, cands), F32),
-        in_specs=[vmem] * 7,
+        in_specs=[vmem] * 9,
         out_specs=vmem,
         scratch_shapes=[
+            pltpu.VMEM((DEPTH, cands), BF16),
+            pltpu.VMEM((feats, DEPTH), BF16),
+            pltpu.VMEM((obs, DEPTH), BF16),
+            pltpu.VMEM((SEG, CHUNK), F32),
+            pltpu.VMEM((DEPTH, FB), F32),
             pltpu.VMEM((slots, feats + obs, CHUNK), BF16),
             pltpu.VMEM((all_samples, feats + obs), BF16),
             pltpu.VMEM((peers_c, samples, feats), BF16),
             pltpu.VMEM((samples, width), BF16),
             pltpu.VMEM((peers_c, samples, width), BF16),
-            pltpu.VMEM((all_samples, feats + obs), F32),
             pltpu.VMEM((peers_r, samples, width), F32),
             pltpu.VMEM((peers_r, samples, width), F32),
             pltpu.VMEM((all_samples, CHUNK), F32),
@@ -320,7 +358,17 @@
         compiler_params=pltpu.CompilerParams(
             collective_id=0, has_side_effects=True, vmem_limit_bytes=56 * 1024 * 1024
         ),
-    )(g, ft, ot, prior_coef, whitened, factor_rows, diag_inv)
+    )(
+        grid_coords,
+        observed,
+        inv_length[:, None],
+        frequencies,
+        phases[None, :],
+        prior_coef,
+        whitened,
+        factor_rows,
+        diag_inv,
+    )
     return out.T
 
 

time: 79.8 us -> 63 us (0.79)
  local copies, waits for them, and re-layouts: 13.3 us -> 3.61 us
  Pallas kernels: 63.7 us -> 59.2 us
  other arithmetic: 2.25 us -> 0 us
    pallas_call x1, Pallas kernels: 63.7 us -> 59.2 us  [body(): pl.pallas_call(functools.partial(kernel, peers_r, peers_c, scale), out_sh...]
    concatenate x3 -> x0, local copies, waits for them, and re-layouts: 3.64 us -> none  [padded(): stacked = jnp.concatenate(rows, axis=0)]
    transpose x2 -> x0, local copies, waits for them, and re-layouts: 2.62 us -> none  [the longest x1 1.94 us: body(): padded(pieces(frequencies * (turn / top)) + pieces(phases[None, :] * turn))]
    unnamed x7 -> x1, local copies, waits for them, and re-layouts: 4.48 us -> 2.27 us
    broadcast_in_dim x2 -> x1, local copies, waits for them, and re-layouts: 0.03 us -> 1.34 us  [body(): inv_length[:, None]]
    reduce_precision x4 -> x0, local copies, waits for them, and re-layouts: 1.14 us -> none  [rounded(): return lax.reduce_precision(a, exponent_bits=8, mantissa_bits=7)]
    pad x1 -> x0, local copies, waits for them, and re-layouts: 1.05 us -> none  [padded(): jnp.pad(stacked, ((0, DEPTH - stacked.shape[0]), (0, 0))).astype(BF16)]
    reduce_sum x2 -> x0, other arithmetic: 1.01 us -> none  [the longest x1 0.89 us: body(): jnp.sum(observed * observed * l2, axis=0, keepdims=True) * (-0.5 * log2e)]
where the time goes in v2:
time: 63 us; the launch traced here: 62.8 us
  Pallas kernels  59.2 us (94%)
  local copies, waits for them, and re-layouts  3.61 us (6%)
    pallas_call x1, Pallas kernels, body(): pl.pallas_call(functools.partial(kernel, peers_r, peers_c, scale), out_sh...  59.2 us
    unnamed x1, local copies, waits for them, and re-layouts  2.27 us
    broadcast_in_dim x1, local copies, waits for them, and re-layouts, body(): inv_length[:, None]  1.34 us

profile of v2, /device:TPU:0, one launch (start us, length us, event | category | flops | bytes accessed | tf_op | source)
XLA Modules:
  0.0 62.8 jit_solution(12961391384375333342)
XLA Ops:
  0.0 1.3 %copy.10.scale_ref = f32[22,1]{1,0:T(8,128)} copy(f32[22,1]{0,1:T(1,128)} %bitcast.5) | data formatting | bytes 176 | tf_op jit(solution)/shard_map/broadcast_in_dim | solution.py:364
  1.3 59.2 %shard_map.91 = f32[64,4096]{1,0:T(8,128)} custom-call(s32[22,4096]{1,0:T(8,128)} %levels_ref.1, f32[22,512]{1,0:T(8,128)} %obs_ref.1, f32[22,1]{1,0:T(8,128)} %copy.10.scale_ref, f32[22,2048]{1,0:T(8,128)} %freq_ref.1, f32[1,2048]{1,0:T(1,128)} %bitcast.4, bf16[32,2048]{1,0:T(8,128)(2,1)} %coef_ref.1, f32[32,512]{1,0:T(8,128)} %x_ref.1, ...), custom_call_target="tpu_custom_call" | custom-call | tf_op jit(solution)/shard_map/pallas_call | solution.py:327
  60.6 2.3 %copy.12 = f32[4096,64]{0,1:T(8,128)} copy(f32[4096,64]{0,1:T(8,128)} %bitcast.3) | data formatting | bytes 2097152
